TPU v7x, 128 devices: a whole 4x4x4 slice. The times are simulated.
128 devices in a mesh: dev: 128 (over y, z, x, core).
Axes of the slice: x: 4, y: 4, z: 4, core: 2. Of those that a mesh axis runs over, the one named last changes fastest.
Arguments:
- upstream: bfloat16 [65536, 1024], P('dev'), may hold values from -24 to 24
- bag: int32 [65536, 8], P('dev'), may hold values from 0 to 767
- next_bag: int32 [65536, 8], P('dev'), may hold values from 0 to 511
- hot_slots: int32 [65536], P('dev'), may hold values from 0 to 8191, as said below
- evict_dest: int32 [128, 128, 2], P('dev'), may hold values from -1 to 1023, as said below
- hot_cache: float32 [65536, 128], P('dev'), may hold values from -6 to 6
- evict_cache: float32 [32768, 128], P('dev'), may hold values from -6 to 6
- hot_table: float32 [8192, 128], P('dev'), may hold values from -6 to 6
- hot_accum: float32 [8192, 128], P('dev'), may hold values from 1 to 100
- owner_table: float32 [131072, 128], P('dev'), may hold values from -6 to 6
- owner_accum: float32 [131072, 128], P('dev'), may hold values from 1 to 30
- cross_w: float32 [2, 1024, 1024], P(None, None, 'dev'), may hold values from -0.1875 to 0.1875
- cross_b: float32 [2, 1024], P(None, 'dev'), may hold values from -3 to 3
- cross_accum: float32 [2, 1024, 1024], P(None, None, 'dev'), may hold values from 10000 to 1000000
Outputs:
- next_first: bfloat16 [65536, 1024], P('dev')
- hot_new: float32 [8192, 128], P('dev')
- hot_accum_new: float32 [8192, 128], P('dev')
- owner_new: float32 [131072, 128], P('dev')
- owner_accum_new: float32 [131072, 128], P('dev')
- cross_w_new: float32 [2, 1024, 1024], P(None, None, 'dev')
- cross_b_new: float32 [2, 1024], P(None, 'dev')
Inputs may be any that keep to these rules, and one draw needn't show every extreme that they name: `hot_slots`: entry d * 512 + 4 * o + k names a row of owner o's block, o * 64 to o * 64 + 63; the 4 rows of one device in one owner's block are distinct. evict_dest[o, s, k] is the row of owner o's block (0 to 1023) that receives the gradient of source s's evicted slot 2 * o + k, or -1 for an empty slot; in each (o, s) bucket the live entries come first, and some bucket is full in every draw.
All inputs are finite; a program needn't handle non-finite values.
Results may differ from a plain program's by a relative error of at most 0.0033.
The roundings to bfloat16 on the way count: a program that leaves them out, or rounds other values in their place, can miss the bound.
Values may be sent and summed in bfloat16 or wider, within the bound.
A program may use at most 128 MiB of HBM per device.

v0:
```python
import jax
import jax.numpy as jnp
from jax import lax
from jax.sharding import PartitionSpec as P

row_rate = 0.05
weight_rate = 0.005
bias_rate = 0.0002
epsilon = 1e-10


def rows_first(arrays, axis, dims):
    turned = [jnp.moveaxis(a, dim, 0) for a, dim in zip(arrays, dims)]
    both = jnp.concatenate([t.reshape(len(t), -1) for t in turned], axis=1)
    filled, at, gathered = (lax.all_gather(both, axis, axis=0, tiled=True), 0, [])
    for t, dim in zip(turned, dims):
        piece = filled[:, at : at + t[0].size].reshape(-1, *t.shape[1:])
        gathered.append(jnp.moveaxis(piece, 0, dim))
        at += t[0].size
    return tuple(gathered)


def adagrad(params, accumulator, gradient, step_rate):
    updated = accumulator + gradient * gradient
    return (params - step_rate * gradient / (jnp.sqrt(updated) + epsilon), updated)


def owner_update(moved, evict_dest, owner_table, owner_accum, width):
    destination = evict_dest[0]
    targets = jnp.where(destination >= 0, destination, owner_table.shape[0]).reshape(-1)
    owner_grad = (
        jnp.zeros(owner_table.shape, jnp.float32)
        .at[targets]
        .add(moved.reshape(-1, width), mode="drop")
    )
    return adagrad(owner_table, owner_accum, owner_grad, row_rate)


def shared_update(arrived_ids, arrived, my_index, hot_table, hot_accum, devices, width):
    block_rows = hot_table.shape[0]
    local_rows = (arrived_ids - my_index * block_rows).reshape(-1)
    block_grad = (
        jnp.zeros(hot_table.shape, jnp.float32).at[local_rows].add(arrived.reshape(-1, width))
    )
    hot_new, hot_accum_new = adagrad(hot_table, hot_accum, block_grad, row_rate)
    returned = jnp.take(hot_new, local_rows, axis=0).reshape(devices, -1, width)
    return (hot_new, hot_accum_new, returned)


def local(
    upstream,
    bag,
    next_bag,
    hot_slots,
    evict_dest,
    hot_cache,
    evict_cache,
    hot_table,
    hot_accum,
    owner_table,
    owner_accum,
    cross_w,
    cross_b,
    cross_accum,
):
    devices = lax.axis_size("dev")
    my_index = lax.axis_index("dev")
    width = hot_cache.shape[1]
    samples = bag.shape[0]
    hot_count = hot_cache.shape[0]
    weights, biases = rows_first(
        (cross_w.astype(jnp.bfloat16), cross_b.astype(jnp.bfloat16)), "dev", (2, 1)
    )
    biases = biases.astype(jnp.float32)
    slot_values = jnp.concatenate([hot_cache, evict_cache], axis=0)
    slot_total = slot_values.shape[0]
    features = jnp.take(slot_values, bag.reshape(-1), axis=0).reshape(samples, -1)
    feat_bf = features.astype(jnp.bfloat16)
    proj_one = jnp.dot(feat_bf, weights[0], preferred_element_type=jnp.float32) + biases[0]
    layer_one = features * proj_one + features
    layer_bf = layer_one.astype(jnp.bfloat16)
    proj_two = jnp.dot(layer_bf, weights[1], preferred_element_type=jnp.float32) + biases[1]
    grad_out = upstream.astype(jnp.float32)
    grad_two = grad_out * features
    grad_two_bf = grad_two.astype(jnp.bfloat16)
    weight_two = jnp.dot(layer_bf.T, grad_two_bf, preferred_element_type=jnp.float32)
    bias_two = jnp.sum(grad_two, axis=0)
    grad_layer = grad_out + jnp.dot(grad_two_bf, weights[1].T, preferred_element_type=jnp.float32)
    grad_one = grad_layer * features
    grad_one_bf = grad_one.astype(jnp.bfloat16)
    weight_one = jnp.dot(feat_bf.T, grad_one_bf, preferred_element_type=jnp.float32)
    bias_one = jnp.sum(grad_one, axis=0)
    weight_shard, bias_shard = (
        lax.psum_scatter(
            jnp.stack([weight_one, weight_two]), "dev", scatter_dimension=2, tiled=True
        ),
        lax.psum_scatter(jnp.stack([bias_one, bias_two]), "dev", scatter_dimension=1, tiled=True),
    )
    grad_feat = grad_out * proj_two + grad_layer * (proj_one + 1.0)
    grad_feat = grad_feat + jnp.dot(grad_one_bf, weights[0].T, preferred_element_type=jnp.float32)
    grad_rows = grad_feat.astype(jnp.bfloat16).reshape(-1, width)
    one_hot = (
        bag.reshape(-1)[:, None]
        == lax.broadcasted_iota(jnp.int32, (grad_rows.shape[0], slot_total), 1)
    ).astype(jnp.bfloat16)
    slot_grad = lax.dot_general(
        one_hot, grad_rows, (((0,), (0,)), ((), ())), preferred_element_type=jnp.float32
    )
    hot_grads = slot_grad[:hot_count].reshape(devices, -1, width)
    evict_grads = slot_grad[hot_count:].reshape(devices, -1, width)
    shared_per = hot_grads.shape[1]
    arrived_ids = lax.all_to_all(
        hot_slots.reshape(devices, -1), "dev", split_axis=0, concat_axis=0, tiled=True
    )
    packed = jnp.concatenate([hot_grads, evict_grads], axis=1)
    unpacked = lax.all_to_all(packed, "dev", split_axis=0, concat_axis=0, tiled=True)
    arrived = unpacked[:, :shared_per]
    moved = unpacked[:, shared_per:]
    hot_new, hot_accum_new, returned = shared_update(
        arrived_ids, arrived, my_index, hot_table, hot_accum, devices, width
    )
    held_rows = lax.all_to_all(returned, "dev", split_axis=0, concat_axis=0, tiled=True).reshape(
        hot_count, width
    )
    owner_new, owner_accum_new = owner_update(moved, evict_dest, owner_table, owner_accum, width)
    cross_w_new, unused = adagrad(cross_w, cross_accum, weight_shard, weight_rate)
    cross_b_new = cross_b - bias_rate * bias_shard
    first_weight, first_bias = rows_first(
        (cross_w_new[0].astype(jnp.bfloat16), cross_b_new[0].astype(jnp.bfloat16)), "dev", (1, 0)
    )
    next_feat = jnp.take(held_rows, next_bag.reshape(-1), axis=0).reshape(next_bag.shape[0], -1)
    proj = jnp.dot(
        next_feat.astype(jnp.bfloat16), first_weight, preferred_element_type=jnp.float32
    ) + first_bias.astype(jnp.float32)
    next_first = (next_feat * proj + next_feat).astype(jnp.bfloat16)
    return (
        next_first,
        hot_new,
        hot_accum_new,
        owner_new,
        owner_accum_new,
        cross_w_new,
        cross_b_new,
    )


def solution(mesh):
    return jax.shard_map(
        local,
        mesh=mesh,
        in_specs=(
            P("dev", None),
            P("dev", None),
            P("dev", None),
            P("dev"),
            P("dev", None, None),
            P("dev", None),
            P("dev", None),
            P("dev", None),
            P("dev", None),
            P("dev", None),
            P("dev", None),
            P(None, None, "dev"),
            P(None, "dev"),
            P(None, None, "dev"),
        ),
        out_specs=(
            P("dev", None),
            P("dev", None),
            P("dev", None),
            P("dev", None),
            P("dev", None),
            P(None, None, "dev"),
            P(None, "dev"),
        ),
        check_vma=False,
    )
```

profile of v0, /device:TPU:1, one launch (start us, length us, event | category | flops | bytes accessed | tf_op | source)
XLA Modules:
  0.0 369.3 jit_solution(14683335172058845515)
XLA Ops:
  7.2 0.8 convert_element_type.76
  8.1 0.7 convert_bitcast_fusion.1
  8.7 0.1 copy.83
  8.8 0.6 pad_maximum_fusion.3
  9.5 0.8 copy.80
  10.4 0.2 reshape.228
  10.6 1.1 pad_maximum_fusion.2
  11.7 14.1 %gather_fusion = f32[4096,128]{1,0:T(8,128)} fusion(f32[768,128]{1,0:T(8,128)S(1)} %pad_maximum_fusion.2, s32[4096]{0:T(1024)S(1)} %broadcast_clamp_fusion.1), kind=kCustom, calls=%fused_computation | custom fusion | bytes 4210688 | tf_op jit(solution)/shard_map/jit(_take)/gather | solution.py:77
  25.7 1.7 gather.21
  27.5 0.2 copy.81
  27.7 2.7 fusion.9
  30.4 51.9 %all-gather.3.cloned.1.call-done = bf16[1024,2050]{1,0:T(8,128)(2,1)} async-done(((bf16[8,2050]{1,0:T(8,128)(2,1)}), bf16[1024,2050]{1,0:T(8,128)(2,1)}) %all-gather.3.cloned.1.call-update) | async-done | bytes 4198416 | tf_op jit(solution)/shard_map/all_gather | solution.py:15
  82.3 4.8 %slice.66 = bf16[1024,2048]{1,0:T(8,128)(2,1)} slice(bf16[1024,2050]{1,0:T(8,128)(2,1)} %all-gather.3.cloned.1.call-done), slice={[0:1024], [0:2048]} | slice | bytes 8388608 | tf_op jit(solution)/shard_map/slice | solution.py:17
  87.1 6.4 %copy.92 = bf16[1024,2048]{0,1:T(8,128)(2,1)} copy(bf16[1024,2048]{1,0:T(8,128)(2,1)} %slice.66) | data formatting | bytes 8388608 | tf_op jit(solution)/shard_map/reshape | solution.py:17
  93.5 1.0 convert_bitcast_fusion
  94.5 0.5 slice_reduce_fusion.1
  95.0 3.3 fusion.11
  98.3 1.6 broadcast_in_dim.51
  100.0 1.7 multiply_reduce_fusion
  101.6 1.4 convolution_bitcast_fusion.1
  103.0 1.7 convolution_bitcast_fusion
  104.7 4.1 %pad_maximum_fusion = f32[2,1024,1024]{2,1,0:T(8,128)} fusion(f32[1,1024,1024]{2,1,0:T(8,128)S(1)} %convolution_bitcast_fusion, f32[1,1024,1024]{2,1,0:T(8,128)S(1)} %convolution_bitcast_fusion.1), kind=kLoop, calls=%fused_computation.7 | loop fusion | flops 2097152 | bytes 16777216 | tf_op jit(solution)/shard_map/stack | solution.py:95
  108.8 13.4 %copy.86 = f32[2,1024,1024]{1,0,2:T(2,128)} copy(f32[2,1024,1024]{2,1,0:T(8,128)} %pad_maximum_fusion) | data formatting | bytes 16777216 | tf_op jit(solution)/shard_map/stack | solution.py:95
  122.3 0.6 copy-done.14
  122.9 0.7 all_to_all.12
  123.6 5.4 %all-to-all-start = ((s32[128,1,4]{2,1,0:T(1,128)}), s32[128,1,4]{2,1,0:T(1,128)S(1)}, u32[]{:S(2)}, u32[]{:S(2)}) async-start(s32[128,1,4]{2,1,0:T(1,128)} %bitcast), calls=%async_computation | async-start | bytes 131072 | tf_op jit(solution)/shard_map/all_to_all | solution.py:112
  129.1 0.1 copy.85
  129.2 0.2 reshape.236
  129.4 68.7 %all-reduce.1 = f32[2,1024]{1,0:T(2,128)S(1)} all-reduce(f32[2,1024]{1,0:T(2,128)S(1)} %pad_maximum_fusion.5), channel_id=3, replica_groups=mesh['dev'=128] {'dev'}, use_global_device_ids=true, to_apply=%region_4.5.clone | all-reduce | flops 2048 | bytes 16384
  198.1 0.6 fusion.35
  198.7 0.1 copy.90
  198.8 82.2 %all-reduce.4.cloned.1.call-done = f32[2,1024,1024]{1,0,2:T(2,128)} async-done(((f32[2,1024,1024]{1,0,2:T(2,128)}), f32[2,1024,1024]{1,0,2:T(2,128)}) %all-reduce.4.cloned.1.call-update) | async-done | bytes 8388624
  281.0 0.8 constant_dynamic-slice_fusion
  282.0 0.6 pad_maximum_fusion.4
  282.6 0.1 copy.91
  282.8 0.1 squeeze.15
  282.9 0.1 eq.10
  283.1 0.2 copy.78
  283.3 0.5 broadcast.169
  283.8 0.8 fusion.37
  284.6 0.1 sub.38
  284.8 3.7 fusion.10
  288.5 0.4 copy-done.4
  288.9 0.2 copy-done.18
  289.1 4.9 %fusion.4 = bf16[512,1024]{1,0:T(8,128)(2,1)} fusion(f32[512,1024]{1,0:T(8,128)S(1)} %fusion.10, bf16[512,1024]{1,0:T(8,128)(2,1)S(1)} %copy-done.18, f32[512,1024]{1,0:T(8,128)S(1)} %copy-done.4, f32[512,1024]{1,0:T(8,128)} %copy-done.19, bf16[2,1024,1024]{2,1,0:T(8,128)(2,1)S(1)} %bitcast.104, f32[1024]{0:T(1024)S(1)} %get-tuple-element.38, ...), kind=kOutput, calls=%fused_computation.18 | convolution fusion | flops 1081081856 | bytes 15216640 | tf_op jit(solution)/shard_map/dot_general | solution.py:82
  294.0 1.5 reshape.231
  295.6 4.0 %fusion = f32[768,128]{1,0:T(8,128)S(1)} fusion(bf16[4096,128]{1,0:T(8,128)(2,1)S(1)} %reshape.231, s32[4096]{0:T(1024)S(1)} %eq.10), kind=kOutput, calls=%fused_computation.6 | convolution fusion | flops 808452096 | bytes 1458176 | tf_op jit(solution)/shard_map/dot_general | solution.py:106
  299.7 0.9 pad_maximum_fusion.1
  300.6 6.6 %all-to-all-start.1 = ((f32[128,6,128]{2,1,0:T(8,128)}), f32[128,6,128]{2,1,0:T(8,128)S(1)}, u32[]{:S(2)}, u32[]{:S(2)}) async-start(f32[128,6,128]{2,1,0:T(8,128)} %pad_maximum_fusion.1), calls=%async_computation.1 | async-start | bytes 1048576 | tf_op jit(solution)/shard_map/all_to_all | solution.py:116
  307.3 13.7 %all-to-all-done.1 = f32[128,6,128]{2,1,0:T(8,128)S(1)} async-done(((f32[128,6,128]{2,1,0:T(8,128)}), f32[128,6,128]{2,1,0:T(8,128)S(1)}, u32[]{:S(2)}, u32[]{:S(2)}) %all-to-all-start.1) | async-done | bytes 393248 | tf_op jit(solution)/shard_map/all_to_all | solution.py:116
  321.0 2.3 scatter_custom_fusion
  323.3 0.6 divide_subtract_fusion.2
  323.9 1.0 gather_fusion.1
  325.0 0.9 broadcast_select_fusion
  325.9 4.6 %all-to-all-start.2 = ((f32[128,4,128]{2,1,0:T(4,128)}), f32[128,4,128]{2,1,0:T(4,128)S(1)}, u32[]{:S(2)}, u32[]{:S(2)}) async-start(f32[128,4,128]{2,1,0:T(4,128)} %broadcast_select_fusion), calls=%async_computation.2 | async-start | bytes 524288 | tf_op jit(solution)/shard_map/all_to_all | solution.py:122
  330.5 0.1 slice.78
  330.5 1.6 scatter_custom_fusion.1
  332.1 1.2 divide_subtract_fusion
  333.3 9.2 %all-to-all-done.2 = f32[128,4,128]{2,1,0:T(4,128)S(1)} async-done(((f32[128,4,128]{2,1,0:T(4,128)}), f32[128,4,128]{2,1,0:T(4,128)S(1)}, u32[]{:S(2)}, u32[]{:S(2)}) %all-to-all-start.2) | async-done | bytes 262176 | tf_op jit(solution)/shard_map/all_to_all | solution.py:122
  342.5 10.8 %gather_fusion.2 = f32[4096,128]{1,0:T(8,128)S(1)} fusion(f32[512,128]{1,0:T(8,128)S(1)} %bitcast.95, s32[4096]{0:T(1024)S(1)} %broadcast_clamp_fusion), kind=kCustom, calls=%fused_computation.2 | custom fusion | bytes 4210688 | tf_op jit(solution)/shard_map/jit(_take)/gather | solution.py:131
  353.3 1.5 gather.26
  354.7 1.1 convert_reduce_fusion
  355.8 1.6 broadcast_in_dim.47
  357.5 5.3 %fusion.6 = bf16[512,1024]{1,0:T(8,128)(2,1)} fusion(f32[512,1024]{1,0:T(8,128)} %gather.26, pred[64,8,8,128]{3,2,1,0:T(8,128)(4,1)S(1)} %bitcast.109, bf16[1024,1025]{1,0:T(8,128)(2,1)} %all-gather.5.cloned.1.call-done, f32[1024]{0:T(1024)S(1)} %convert_reduce_fusion), kind=kOutput, calls=%fused_computation.20 | convolution fusion | flops 1077411840 | bytes 8392704 | tf_op jit(solution)/shard_map/dot_general | solution.py:132
  (62 shorter events, 0.5 us)
Async XLA Ops:
  7.2 75.1 %all-gather.3.cloned.1.call-start = ((), (), s32[]{:S(2)}) async-start(), calls=%async_computation.3 | async-start | bytes 4491264 | tf_op jit(solution)/shard_map/all_gather | solution.py:15
  9.5 271.6 %all-reduce.4.cloned.1.call-start = ((), (), s32[]{:S(2)}) async-start(), calls=%async_computation.5 | async-start | bytes 16777216
  25.7 1.7 copy-start.9
  95.0 5.0 %copy-start.1 = (bf16[1024,2048]{0,1:T(8,128)(2,1)S(1)}, bf16[1024,2048]{0,1:T(8,128)(2,1)}, u32[]{:S(2)}) copy-start(bf16[1024,2048]{0,1:T(8,128)(2,1)} %copy.92) | copy-start | bytes 12582916
  95.0 5.0 %copy-start.17 = (bf16[512,1024]{1,0:T(8,128)(2,1)S(1)}, bf16[512,1024]{1,0:T(8,128)(2,1)}, u32[]{:S(2)}) copy-start(bf16[512,1024]{1,0:T(8,128)(2,1)} %param.14) | copy-start | bytes 3145732
  98.3 4.7 %copy-start.19 = (f32[512,1024]{1,0:T(8,128)}, f32[512,1024]{1,0:T(8,128)S(1)}, u32[]{:S(2)}) copy-start(f32[512,1024]{1,0:T(8,128)S(1)} %fusion.11) | copy-start | bytes 6291460
  101.6 1.4 copy-start.3
  122.2 0.7 copy-start.14
  122.2 6.9 %copy-start.10 = (s32[512,8]{0,1:T(8,128)S(1)}, s32[512,8]{0,1:T(8,128)}, u32[]{:S(2)}) copy-start(s32[512,8]{0,1:T(8,128)} %param.16) | copy-start | bytes 49156
  122.2 75.9 %copy-start.16 = (f32[2,8]{1,0:T(2,128)S(1)}, f32[2,8]{1,0:T(2,128)}, u32[]{:S(2)}) copy-start(f32[2,8]{1,0:T(2,128)} %param.26) | copy-start | bytes 196
  122.2 159.7 %copy-start.7 = (f32[2,1024,8]{1,2,0:T(8,128)S(1)}, f32[2,1024,8]{1,2,0:T(8,128)}, u32[]{:S(2)}) copy-start(f32[2,1024,8]{1,2,0:T(8,128)} %param.25) | copy-start | bytes 196612
  122.2 159.7 %copy-start.11 = (f32[2,1024,8]{1,2,0:T(8,128)S(1)}, f32[2,1024,8]{1,2,0:T(8,128)}, u32[]{:S(2)}) copy-start(f32[2,1024,8]{1,2,0:T(8,128)} %param.27) | copy-start | bytes 196612
  122.2 160.4 %copy-start.15 = (s32[1,128,2]{1,2,0:T(2,128)S(1)}, s32[1,128,2]{1,2,0:T(2,128)}, u32[]{:S(2)}) copy-start(s32[1,128,2]{1,2,0:T(2,128)} %param.18) | copy-start | bytes 3076
  123.6 159.7 %all-to-all-start = ((s32[128,1,4]{2,1,0:T(1,128)}), s32[128,1,4]{2,1,0:T(1,128)S(1)}, u32[]{:S(2)}, u32[]{:S(2)}) async-start(s32[128,1,4]{2,1,0:T(1,128)} %bitcast), calls=%async_computation | async-start | bytes 131072 | tf_op jit(solution)/shard_map/all_to_all | solution.py:112
  129.0 225.7 %all-gather.5.cloned.1.call-start = ((), (), s32[]{:S(2)}) async-start(), calls=%async_computation.4 | async-start | bytes 2377728 | tf_op jit(solution)/shard_map/all_gather | solution.py:15
  282.0 6.5 %copy-start.8 = (f32[2,1024,8]{1,2,0:T(8,128)}, f32[2,1024,8]{1,2,0:T(8,128)S(1)}, u32[]{:S(2)}) copy-start(f32[2,1024,8]{1,2,0:T(8,128)S(1)} %divide_subtract_fusion.1) | copy-start | bytes 196612
  284.7 3.7 %copy-start.2 = (bf16[1024,2048]{0,1:T(8,128)(2,1)S(1)}, bf16[1024,2048]{0,1:T(8,128)(2,1)}, u32[]{:S(2)}) copy-start(bf16[1024,2048]{0,1:T(8,128)(2,1)} %copy.92) | copy-start | bytes 12582916
  284.8 4.1 %copy-start.4 = (f32[512,1024]{1,0:T(8,128)S(1)}, f32[512,1024]{1,0:T(8,128)}, u32[]{:S(2)}) copy-start(f32[512,1024]{1,0:T(8,128)} %copy-done.3) | copy-start | bytes 6291460
  284.8 4.3 %copy-start.18 = (bf16[512,1024]{1,0:T(8,128)(2,1)S(1)}, bf16[512,1024]{1,0:T(8,128)(2,1)}, u32[]{:S(2)}) copy-start(bf16[512,1024]{1,0:T(8,128)(2,1)} %param.14) | copy-start | bytes 3145732
  299.6 23.7 %copy-start.12 = (f32[64,128]{1,0:T(8,128)S(1)}, f32[64,128]{1,0:T(8,128)}, u32[]{:S(2)}) copy-start(f32[64,128]{1,0:T(8,128)} %param.21) | copy-start | bytes 98308
  299.6 23.6 %copy-start.13 = (f32[64,128]{1,0:T(8,128)S(1)}, f32[64,128]{1,0:T(8,128)}, u32[]{:S(2)}) copy-start(f32[64,128]{1,0:T(8,128)} %param.22) | copy-start | bytes 98308
  300.6 20.4 %all-to-all-start.1 = ((f32[128,6,128]{2,1,0:T(8,128)}), f32[128,6,128]{2,1,0:T(8,128)S(1)}, u32[]{:S(2)}, u32[]{:S(2)}) async-start(f32[128,6,128]{2,1,0:T(8,128)} %pad_maximum_fusion.1), calls=%async_computation.1 | async-start | bytes 1048576 | tf_op jit(solution)/shard_map/all_to_all | solution.py:116
  323.9 8.2 %copy-start = (f32[64,128]{1,0:T(8,128)}, f32[64,128]{1,0:T(8,128)S(1)}, u32[]{:S(2)}) copy-start(f32[64,128]{1,0:T(8,128)S(1)} %get-tuple-element.43) | copy-start | bytes 98308
  323.9 8.2 %copy-start.5 = (f32[1024,128]{1,0:T(8,128)S(1)}, f32[1024,128]{1,0:T(8,128)}, u32[]{:S(2)}) copy-start(f32[1024,128]{1,0:T(8,128)} %param.23) | copy-start | bytes 1572868
  323.9 8.2 %copy-start.6 = (f32[1024,128]{1,0:T(8,128)S(1)}, f32[1024,128]{1,0:T(8,128)}, u32[]{:S(2)}) copy-start(f32[1024,128]{1,0:T(8,128)} %param.24) | copy-start | bytes 1572868
  325.9 16.6 %all-to-all-start.2 = ((f32[128,4,128]{2,1,0:T(4,128)}), f32[128,4,128]{2,1,0:T(4,128)S(1)}, u32[]{:S(2)}, u32[]{:S(2)}) async-start(f32[128,4,128]{2,1,0:T(4,128)} %broadcast_select_fusion), calls=%async_computation.2 | async-start | bytes 524288 | tf_op jit(solution)/shard_map/all_to_all | solution.py:122
Sparse Core Ops, SparseCore 0:
  11.7 70.5 all-gather.2
  122.4 158.6 all-reduce.3
  284.4 65.2 all-gather.4
where the time goes:
time: 370 us; the launch traced here: 369 us
  waiting for transfers between devices  157 us (42%)
  blocking collectives  68.7 us (19%)
  local copies, waits for them, and re-layouts  64.8 us (18%)
  matrix products  26 us (7%)
  other arithmetic  21.8 us (6%)
  starting transfers between devices  16.7 us (5%)
  between operations  14.3 us (4%)
    unnamed x4, waiting for transfers between devices  82.3 us
    unnamed x1, blocking collectives  68.7 us
    all_gather x2, waiting for transfers between devices, rows_first(): lax.all_gather(both, axis, axis=0, tiled=True)  51.9 us
    gather x2, local copies, waits for them, and re-layouts, local(): jnp.take(slot_values, bag.reshape(-1), axis=0).reshape(samples, -1)  15.8 us
    all_to_all x1, waiting for transfers between devices, local(): lax.all_to_all(packed, 'dev', split_axis=0, concat_axis=0, tiled=True)  13.7 us
    another operation x1, local copies, waits for them, and re-layouts, local(): jnp.stack([weight_one, weight_two])  13.4 us
    gather x2, local copies, waits for them, and re-layouts, local(): jnp.take(held_rows, next_bag.reshape(-1), axis=0)  12.2 us
    all_to_all x1, waiting for transfers between devices, local(): lax.all_to_all(returned, 'dev', split_axis=0, concat_axis=0, tiled=True)  9.17 us
  transfers between devices with their start and end apart: 6, of which 4 were waited for; matrix products, arithmetic and copies ran while one was open for 16% of the time, Pallas kernels for 0%

commit v1 on v0

--- a/solution.py
+++ b/solution.py
@@ -12,7 +12,13 @@
 def rows_first(arrays, axis, dims):
     turned = [jnp.moveaxis(a, dim, 0) for a, dim in zip(arrays, dims)]
     both = jnp.concatenate([t.reshape(len(t), -1) for t in turned], axis=1)
-    filled, at, gathered = (lax.all_gather(both, axis, axis=0, tiled=True), 0, [])
+    filled, at, gathered = (
+        jnp.concatenate(
+            lax.all_to_all(jnp.stack([both] * lax.axis_size(axis)), axis, 0, 0), axis=0
+        ),
+        0,
+        [],
+    )
     for t, dim in zip(turned, dims):
         piece = filled[:, at : at + t[0].size].reshape(-1, *t.shape[1:])
         gathered.append(jnp.moveaxis(piece, 0, dim))

time: 370 us -> 338 us (0.914)
  waiting for transfers between devices: 157 us -> 107 us
  starting transfers between devices: 16.7 us -> 33.2 us
  local copies, waits for them, and re-layouts: 64.8 us -> 68.5 us
    all_to_all x0 -> x2, waiting for transfers between devices: none -> 53.2 us  [rows_first(): lax.all_to_all(jnp.stack([both] * lax.axis_size(axis)), axis, 0, 0)]
    all_gather x2 -> x0, waiting for transfers between devices: 51.9 us -> none  [rows_first(): lax.all_gather(both, axis, axis=0, tiled=True)]
    unnamed x4 -> x2, waiting for transfers between devices: 82.3 us -> 44.4 us
    all_to_all x0 -> x2, starting transfers between devices: none -> 18.9 us  [rows_first(): lax.all_to_all(jnp.stack([both] * lax.axis_size(axis)), axis, 0, 0)]
    all_to_all x1, waiting for transfers between devices: 13.7 us -> 0.01 us  [local(): lax.all_to_all(packed, 'dev', split_axis=0, concat_axis=0, tiled=True)]
    all_to_all x1, waiting for transfers between devices: 0.01 us -> 9.27 us  [local(): lax.all_to_all(hot_slots.reshape(devices, -1), 'dev', split_axis=0, conca...]
    all_to_all x1, waiting for transfers between devices: 9.17 us -> 0.01 us  [local(): lax.all_to_all(returned, 'dev', split_axis=0, concat_axis=0, tiled=True)]
    another operation x0 -> x2, local copies, waits for them, and re-layouts: none -> 3.99 us  [rows_first(): jnp.stack([both] * lax.axis_size(axis))]
  transfers between devices with their start and end apart: 6 -> 6, of which waited for: 4 -> 4; matrix products, arithmetic and copies ran while one was open for 16% -> 17% of each run, Pallas kernels for 0% -> 0%
where the time goes in v1:
time: 338 us; the launch traced here: 337 us
  waiting for transfers between devices  107 us (32%)
  local copies, waits for them, and re-layouts  68.5 us (20%)
  blocking collectives  68.2 us (20%)
  starting transfers between devices  33.2 us (10%)
  matrix products  26.3 us (8%)
  other arithmetic  19.5 us (6%)
  between operations  14.6 us (4%)
    unnamed x1, blocking collectives  68.2 us
    all_to_all x2, waiting for transfers between devices, rows_first(): lax.all_to_all(jnp.stack([both] * lax.axis_size(axis)), axis, 0, 0)  53.2 us
    unnamed x2, waiting for transfers between devices  44.4 us
    all_to_all x2, starting transfers between devices, rows_first(): lax.all_to_all(jnp.stack([both] * lax.axis_size(axis)), axis, 0, 0)  18.9 us
    gather x2, local copies, waits for them, and re-layouts, local(): jnp.take(slot_values, bag.reshape(-1), axis=0).reshape(samples, -1)  15.8 us
    another operation x1, local copies, waits for them, and re-layouts, local(): jnp.stack([weight_one, weight_two])  13.4 us
    gather x2, local copies, waits for them, and re-layouts, local(): jnp.take(held_rows, next_bag.reshape(-1), axis=0)  12.3 us
    all_to_all x1, waiting for transfers between devices, local(): lax.all_to_all(hot_slots.reshape(devices, -1), 'dev', split_axis=0, conca...  9.27 us
  transfers between devices with their start and end apart: 6, of which 4 were waited for; matrix products, arithmetic and copies ran while one was open for 17% of the time, Pallas kernels for 0%

profile of v1, /device:TPU:1, one launch (start us, length us, event | category | flops | bytes accessed | tf_op | source)
XLA Modules:
  0.0 337.2 jit_solution(15459773273837228570)
XLA Ops:
  7.2 0.8 convert_element_type.76
  8.0 0.7 convert_bitcast_fusion.1
  8.7 0.1 copy.85
  8.8 2.4 stack.16
  11.2 11.9 %all-to-all-start.1 = ((bf16[128,8,2050]{2,1,0:T(8,128)(2,1)}), bf16[128,8,2050]{2,1,0:T(8,128)(2,1)}, u32[]{:S(2)}, u32[]{:S(2)}) async-start(bf16[128,8,2050]{2,1,0:T(8,128)(2,1)} %stack.16), calls=%async_computation.1 | async-start | bytes 8912896 | tf_op jit(solution)/shard_map/all_to_all | solution.py:17
  23.2 0.1 copy.82
  23.3 0.2 reshape.238
  23.6 14.1 %gather_fusion = f32[4096,128]{1,0:T(8,128)} fusion(f32[768,128]{1,0:T(8,128)S(1)} %pad_maximum_fusion.2, s32[4096]{0:T(1024)S(1)} %broadcast_clamp_fusion.1), kind=kCustom, calls=%fused_computation | custom fusion | bytes 4210688 | tf_op jit(solution)/shard_map/jit(_take)/gather | solution.py:83
  37.7 1.7 gather.21
  39.4 0.2 copy.83
  39.6 2.7 fusion.9
  42.3 36.3 %all-to-all-done.1 = bf16[128,8,2050]{2,1,0:T(8,128)(2,1)} async-done(((bf16[128,8,2050]{2,1,0:T(8,128)(2,1)}), bf16[128,8,2050]{2,1,0:T(8,128)(2,1)}, u32[]{:S(2)}, u32[]{:S(2)}) %all-to-all-start.1) | async-done | bytes 4198432 | tf_op jit(solution)/shard_map/all_to_all | solution.py:17
  78.6 4.8 %slice.66 = bf16[1024,2048]{1,0:T(8,128)(2,1)} slice(bf16[1024,2050]{1,0:T(8,128)(2,1)} %bitcast.8), slice={[0:1024], [0:2048]} | slice | bytes 8388608 | tf_op jit(solution)/shard_map/slice | solution.py:23
  83.4 1.0 convert_bitcast_fusion
  84.4 6.4 %copy.94 = bf16[1024,2048]{0,1:T(8,128)(2,1)} copy(bf16[1024,2048]{1,0:T(8,128)(2,1)} %slice.66) | data formatting | bytes 8388608 | tf_op jit(solution)/shard_map/reshape | solution.py:23
  90.8 0.5 slice_reduce_fusion.1
  91.3 3.3 fusion.11
  94.6 1.6 broadcast_in_dim.51
  96.3 1.7 multiply_reduce_fusion
  97.9 1.4 convolution_bitcast_fusion.1
  99.3 1.7 convolution_bitcast_fusion
  101.0 4.1 %pad_maximum_fusion = f32[2,1024,1024]{2,1,0:T(8,128)} fusion(f32[1,1024,1024]{2,1,0:T(8,128)S(1)} %convolution_bitcast_fusion, f32[1,1024,1024]{2,1,0:T(8,128)S(1)} %convolution_bitcast_fusion.1), kind=kLoop, calls=%fused_computation.7 | loop fusion | flops 2097152 | bytes 16777216 | tf_op jit(solution)/shard_map/stack | solution.py:101
  105.1 13.4 %copy.88 = f32[2,1024,1024]{1,0,2:T(2,128)} copy(f32[2,1024,1024]{2,1,0:T(8,128)} %pad_maximum_fusion) | data formatting | bytes 16777216 | tf_op jit(solution)/shard_map/stack | solution.py:101
  118.5 0.7 copy-done.16
  119.2 0.7 all_to_all.18
  119.9 4.8 %all-to-all-start = ((s32[128,1,4]{2,1,0:T(1,128)}), s32[128,1,4]{2,1,0:T(1,128)S(1)}, u32[]{:S(2)}, u32[]{:S(2)}) async-start(s32[128,1,4]{2,1,0:T(1,128)} %bitcast), calls=%async_computation | async-start | bytes 131072 | tf_op jit(solution)/shard_map/all_to_all | solution.py:118
  124.7 0.1 eq.10
  124.9 9.3 %all-to-all-done = s32[128,1,4]{2,1,0:T(1,128)S(1)} async-done(((s32[128,1,4]{2,1,0:T(1,128)}), s32[128,1,4]{2,1,0:T(1,128)S(1)}, u32[]{:S(2)}, u32[]{:S(2)}) %all-to-all-start) | async-done | bytes 2080 | tf_op jit(solution)/shard_map/all_to_all | solution.py:118
  134.2 0.5 broadcast.173
  134.7 0.8 fusion.37
  135.5 0.1 sub.38
  135.7 3.8 %fusion.10 = f32[512,1024]{1,0:T(8,128)S(1)} fusion(bf16[2,1024,1024]{2,1,0:T(8,128)(2,1)} %bitcast.104, f32[512,1024]{1,0:T(8,128)} %copy-done.3, f32[512,1024]{1,0:T(8,128)S(1)} %gather.21, pred[64,8,8,128]{3,2,1,0:T(8,128)(4,1)S(1)} %bitcast.101), kind=kOutput, calls=%fused_computation.29 | convolution fusion | flops 1075314688 | bytes 8912896 | tf_op jit(solution)/shard_map/dot_general | solution.py:106
  139.6 0.6 copy-done.4
  140.2 0.2 copy-done.20
  140.4 5.1 %fusion.4 = bf16[512,1024]{1,0:T(8,128)(2,1)} fusion(f32[512,1024]{1,0:T(8,128)S(1)} %fusion.10, bf16[512,1024]{1,0:T(8,128)(2,1)S(1)} %copy-done.20, f32[512,1024]{1,0:T(8,128)S(1)} %copy-done.4, f32[512,1024]{1,0:T(8,128)} %copy-done.21, bf16[2,1024,1024]{2,1,0:T(8,128)(2,1)S(1)} %bitcast.106, f32[1024]{0:T(1024)S(1)} %get-tuple-element.38, ...), kind=kOutput, calls=%fused_computation.18 | convolution fusion | flops 1081081856 | bytes 15216640 | tf_op jit(solution)/shard_map/dot_general | solution.py:88
  145.5 1.5 reshape.242
  147.1 4.0 %fusion = f32[768,128]{1,0:T(8,128)S(1)} fusion(bf16[4096,128]{1,0:T(8,128)(2,1)S(1)} %reshape.242, s32[4096]{0:T(1024)S(1)} %eq.10), kind=kOutput, calls=%fused_computation.6 | convolution fusion | flops 808452096 | bytes 1458176 | tf_op jit(solution)/shard_map/dot_general | solution.py:112
  151.2 0.9 pad_maximum_fusion.1
  152.1 4.6 %all-to-all-start.2 = ((f32[128,6,128]{2,1,0:T(8,128)}), f32[128,6,128]{2,1,0:T(8,128)S(1)}, u32[]{:S(2)}, u32[]{:S(2)}) async-start(f32[128,6,128]{2,1,0:T(8,128)} %pad_maximum_fusion.1), calls=%async_computation.2 | async-start | bytes 1048576 | tf_op jit(solution)/shard_map/all_to_all | solution.py:122
  156.8 68.2 %all-reduce.1 = f32[2,1024]{1,0:T(2,128)S(1)} all-reduce(f32[2,1024]{1,0:T(2,128)S(1)} %pad_maximum_fusion.5), channel_id=3, replica_groups=mesh['dev'=128] {'dev'}, use_global_device_ids=true, to_apply=%region_4.5.clone | all-reduce | flops 2048 | bytes 16384
  225.0 0.6 fusion.35
  225.6 0.1 copy.92
  225.8 2.3 scatter_custom_fusion
  228.1 0.6 divide_subtract_fusion.2
  228.7 1.0 gather_fusion.1
  229.7 0.9 broadcast_select_fusion
  230.6 4.7 %all-to-all-start.3 = ((f32[128,4,128]{2,1,0:T(4,128)}), f32[128,4,128]{2,1,0:T(4,128)S(1)}, u32[]{:S(2)}, u32[]{:S(2)}) async-start(f32[128,4,128]{2,1,0:T(4,128)} %broadcast_select_fusion), calls=%async_computation.3 | async-start | bytes 524288 | tf_op jit(solution)/shard_map/all_to_all | solution.py:128
  235.4 44.4 %all-reduce.4.cloned.1.call-done = f32[2,1024,1024]{1,0,2:T(2,128)} async-done(((f32[2,1024,1024]{1,0,2:T(2,128)}), f32[2,1024,1024]{1,0,2:T(2,128)}) %all-reduce.4.cloned.1.call-update) | async-done | bytes 8388624
  279.8 0.8 constant_dynamic-slice_fusion
  280.7 1.6 stack.23
  282.4 7.0 %all-to-all-start.4 = ((bf16[128,8,1025]{2,1,0:T(8,128)(2,1)}), bf16[128,8,1025]{2,1,0:T(8,128)(2,1)}, u32[]{:S(2)}, u32[]{:S(2)}) async-start(bf16[128,8,1025]{2,1,0:T(8,128)(2,1)} %stack.23), calls=%async_computation.4 | async-start | bytes 4718592 | tf_op jit(solution)/shard_map/all_to_all | solution.py:17
  289.4 0.1 copy.87
  289.5 0.2 reshape.247
  289.7 0.2 copy.80
  289.9 0.1 copy.93
  290.0 0.1 squeeze.15
  290.3 1.6 scatter_custom_fusion.1
  291.9 1.2 divide_subtract_fusion
  293.1 10.8 %gather_fusion.2 = f32[4096,128]{1,0:T(8,128)S(1)} fusion(f32[512,128]{1,0:T(8,128)S(1)} %bitcast.97, s32[4096]{0:T(1024)S(1)} %broadcast_clamp_fusion), kind=kCustom, calls=%fused_computation.2 | custom fusion | bytes 4210688 | tf_op jit(solution)/shard_map/jit(_take)/gather | solution.py:137
  303.8 1.6 gather.26
  305.4 16.9 %all-to-all-done.4 = bf16[128,8,1025]{2,1,0:T(8,128)(2,1)} async-done(((bf16[128,8,1025]{2,1,0:T(8,128)(2,1)}), bf16[128,8,1025]{2,1,0:T(8,128)(2,1)}, u32[]{:S(2)}, u32[]{:S(2)}) %all-to-all-start.4) | async-done | bytes 2099232 | tf_op jit(solution)/shard_map/all_to_all | solution.py:17
  322.3 1.1 convert_reduce_fusion
  323.4 1.6 broadcast_in_dim.47
  325.1 5.3 %fusion.6 = bf16[512,1024]{1,0:T(8,128)(2,1)} fusion(f32[512,1024]{1,0:T(8,128)} %gather.26, pred[64,8,8,128]{3,2,1,0:T(8,128)(4,1)S(1)} %bitcast.111, bf16[1024,1025]{1,0:T(8,128)(2,1)} %bitcast.28, f32[1024]{0:T(1024)S(1)} %convert_reduce_fusion), kind=kOutput, calls=%fused_computation.20 | convolution fusion | flops 1077411840 | bytes 8392704 | tf_op jit(solution)/shard_map/dot_general | solution.py:138
  (66 shorter events, 0.5 us)
Async XLA Ops:
  11.2 12.0 %copy-start.11 = (s32[512,8]{0,1:T(8,128)S(1)}, s32[512,8]{0,1:T(8,128)}, u32[]{:S(2)}) copy-start(s32[512,8]{0,1:T(8,128)} %param.15) | copy-start | bytes 49156
  11.2 12.3 %copy-start.7 = (f32[512,128]{1,0:T(8,128)S(1)}, f32[512,128]{1,0:T(8,128)}, u32[]{:S(2)}) copy-start(f32[512,128]{1,0:T(8,128)} %param.19) | copy-start | bytes 786436
  11.2 12.3 %copy-start.9 = (f32[256,128]{1,0:T(8,128)S(1)}, f32[256,128]{1,0:T(8,128)}, u32[]{:S(2)}) copy-start(f32[256,128]{1,0:T(8,128)} %param.20) | copy-start | bytes 393220
  11.2 67.4 %all-to-all-start.1 = ((bf16[128,8,2050]{2,1,0:T(8,128)(2,1)}), bf16[128,8,2050]{2,1,0:T(8,128)(2,1)}, u32[]{:S(2)}, u32[]{:S(2)}) async-start(bf16[128,8,2050]{2,1,0:T(8,128)(2,1)} %stack.16), calls=%async_computation.1 | async-start | bytes 8912896 | tf_op jit(solution)/shard_map/all_to_all | solution.py:17
  23.1 256.7 %all-reduce.4.cloned.1.call-start = ((), (), s32[]{:S(2)}) async-start(), calls=%async_computation.5 | async-start | bytes 16777216
  91.3 5.0 %copy-start.1 = (bf16[1024,2048]{0,1:T(8,128)(2,1)S(1)}, bf16[1024,2048]{0,1:T(8,128)(2,1)}, u32[]{:S(2)}) copy-start(bf16[1024,2048]{0,1:T(8,128)(2,1)} %copy.94) | copy-start | bytes 12582916
  91.3 5.0 %copy-start.19 = (bf16[512,1024]{1,0:T(8,128)(2,1)S(1)}, bf16[512,1024]{1,0:T(8,128)(2,1)}, u32[]{:S(2)}) copy-start(bf16[512,1024]{1,0:T(8,128)(2,1)} %param.14) | copy-start | bytes 3145732
  94.6 4.7 %copy-start.21 = (f32[512,1024]{1,0:T(8,128)}, f32[512,1024]{1,0:T(8,128)S(1)}, u32[]{:S(2)}) copy-start(f32[512,1024]{1,0:T(8,128)S(1)} %fusion.11) | copy-start | bytes 6291460
  97.9 1.4 copy-start.3
  118.5 0.7 copy-start.16
  119.9 14.3 %all-to-all-start = ((s32[128,1,4]{2,1,0:T(1,128)}), s32[128,1,4]{2,1,0:T(1,128)S(1)}, u32[]{:S(2)}, u32[]{:S(2)}) async-start(s32[128,1,4]{2,1,0:T(1,128)} %bitcast), calls=%async_computation | async-start | bytes 131072 | tf_op jit(solution)/shard_map/all_to_all | solution.py:118
  135.7 3.9 %copy-start.2 = (bf16[1024,2048]{0,1:T(8,128)(2,1)S(1)}, bf16[1024,2048]{0,1:T(8,128)(2,1)}, u32[]{:S(2)}) copy-start(bf16[1024,2048]{0,1:T(8,128)(2,1)} %copy.94) | copy-start | bytes 12582916
  135.7 4.5 %copy-start.4 = (f32[512,1024]{1,0:T(8,128)S(1)}, f32[512,1024]{1,0:T(8,128)}, u32[]{:S(2)}) copy-start(f32[512,1024]{1,0:T(8,128)} %copy-done.3) | copy-start | bytes 6291460
  135.7 4.7 %copy-start.20 = (bf16[512,1024]{1,0:T(8,128)(2,1)S(1)}, bf16[512,1024]{1,0:T(8,128)(2,1)}, u32[]{:S(2)}) copy-start(bf16[512,1024]{1,0:T(8,128)(2,1)} %param.14) | copy-start | bytes 3145732
  151.1 73.9 %copy-start.18 = (f32[2,8]{1,0:T(2,128)S(1)}, f32[2,8]{1,0:T(2,128)}, u32[]{:S(2)}) copy-start(f32[2,8]{1,0:T(2,128)} %param.26) | copy-start | bytes 196
  151.1 76.9 %copy-start.14 = (f32[64,128]{1,0:T(8,128)S(1)}, f32[64,128]{1,0:T(8,128)}, u32[]{:S(2)}) copy-start(f32[64,128]{1,0:T(8,128)} %param.21) | copy-start | bytes 98308
  151.1 76.9 %copy-start.15 = (f32[64,128]{1,0:T(8,128)S(1)}, f32[64,128]{1,0:T(8,128)}, u32[]{:S(2)}) copy-start(f32[64,128]{1,0:T(8,128)} %param.22) | copy-start | bytes 98308
  152.1 73.6 %all-to-all-start.2 = ((f32[128,6,128]{2,1,0:T(8,128)}), f32[128,6,128]{2,1,0:T(8,128)S(1)}, u32[]{:S(2)}, u32[]{:S(2)}) async-start(f32[128,6,128]{2,1,0:T(8,128)} %pad_maximum_fusion.1), calls=%async_computation.2 | async-start | bytes 1048576 | tf_op jit(solution)/shard_map/all_to_all | solution.py:122
  225.7 54.9 %copy-start.8 = (f32[2,1024,8]{1,2,0:T(8,128)S(1)}, f32[2,1024,8]{1,2,0:T(8,128)}, u32[]{:S(2)}) copy-start(f32[2,1024,8]{1,2,0:T(8,128)} %param.25) | copy-start | bytes 196612
  225.7 54.9 %copy-start.13 = (f32[2,1024,8]{1,2,0:T(8,128)S(1)}, f32[2,1024,8]{1,2,0:T(8,128)}, u32[]{:S(2)}) copy-start(f32[2,1024,8]{1,2,0:T(8,128)} %param.27) | copy-start | bytes 196612
  228.7 53.6 %copy-start = (f32[64,128]{1,0:T(8,128)}, f32[64,128]{1,0:T(8,128)S(1)}, u32[]{:S(2)}) copy-start(f32[64,128]{1,0:T(8,128)S(1)} %get-tuple-element.43) | copy-start | bytes 98308
  230.6 50.1 %all-to-all-start.3 = ((f32[128,4,128]{2,1,0:T(4,128)}), f32[128,4,128]{2,1,0:T(4,128)S(1)}, u32[]{:S(2)}, u32[]{:S(2)}) async-start(f32[128,4,128]{2,1,0:T(4,128)} %broadcast_select_fusion), calls=%async_computation.3 | async-start | bytes 524288 | tf_op jit(solution)/shard_map/all_to_all | solution.py:128
  280.7 1.6 copy-start.10
  282.3 7.1 %copy-start.12 = (s32[512,8]{0,1:T(8,128)S(1)}, s32[512,8]{0,1:T(8,128)}, u32[]{:S(2)}) copy-start(s32[512,8]{0,1:T(8,128)} %param.16) | copy-start | bytes 49156
  282.3 7.6 %copy-start.17 = (s32[1,128,2]{1,2,0:T(2,128)S(1)}, s32[1,128,2]{1,2,0:T(2,128)}, u32[]{:S(2)}) copy-start(s32[1,128,2]{1,2,0:T(2,128)} %param.18) | copy-start | bytes 3076
  282.3 9.5 %copy-start.5 = (f32[1024,128]{1,0:T(8,128)S(1)}, f32[1024,128]{1,0:T(8,128)}, u32[]{:S(2)}) copy-start(f32[1024,128]{1,0:T(8,128)} %param.23) | copy-start | bytes 1572868
  282.3 9.5 %copy-start.6 = (f32[1024,128]{1,0:T(8,128)S(1)}, f32[1024,128]{1,0:T(8,128)}, u32[]{:S(2)}) copy-start(f32[1024,128]{1,0:T(8,128)} %param.24) | copy-start | bytes 1572868
  282.4 40.0 %all-to-all-start.4 = ((bf16[128,8,1025]{2,1,0:T(8,128)(2,1)}), bf16[128,8,1025]{2,1,0:T(8,128)(2,1)}, u32[]{:S(2)}, u32[]{:S(2)}) async-start(bf16[128,8,1025]{2,1,0:T(8,128)(2,1)} %stack.23), calls=%async_computation.4 | async-start | bytes 4718592 | tf_op jit(solution)/shard_map/all_to_all | solution.py:17
Sparse Core Ops, SparseCore 0:
  118.6 161.0 all-reduce.3
